TPU v7x, 32 devices: a whole 2x2x4 slice. The times are simulated.
32 devices in a mesh: grp: 4 (over z), mem: 8 (over y, x, core).
Axes of the slice: x: 2, y: 2, z: 4, core: 2. Of those that a mesh axis runs over, the one named last changes fastest.
Arguments:
- spectra: bfloat16 [128, 8, 2, 1024], P(('grp', 'mem')), may hold values from -6 to 6
- seg_mask: int32 [128, 8], P(('grp', 'mem')), may hold values 0 or 1
- chan_pos: int32 [128], P(('grp', 'mem')), may hold values from 0 to 127, each once
Outputs:
- correlations: bfloat16 [128, 4, 32, 128], P('grp', None, 'mem')
Inputs may be any that keep to these rules, and one draw needn't show every extreme that they name: `seg_mask`: segment validity is 0 or 1. `chan_pos`: each position appears once.
All inputs are finite; a program needn't handle non-finite values. No bound on the sum of `seg_mask` on one device may be relied on, other than what follows from the above.
Results may differ from a plain program's by a relative error of at most 0.0045.
Values may be sent and summed in bfloat16 or wider, within the bound.
A program may use at most 128 MiB of HBM per device.

v0:
```python
import math
import jax
import jax.numpy as jnp
from jax import lax
from jax.sharding import PartitionSpec as P

BINS = 1024
LAGS = 128


def make_table(bins, lags):
    freq = jnp.arange(bins, dtype=jnp.int32)
    lag_ids = jnp.arange(lags, dtype=jnp.int32) - lags // 2
    phase = jnp.mod(freq[:, None] * lag_ids[None, :], bins).astype(jnp.float32) * (
        2.0 * math.pi / bins
    )
    table = jnp.concatenate([jnp.cos(phase), -jnp.sin(phase)], axis=0).astype(jnp.bfloat16)
    return (table, lag_ids.astype(jnp.float32))


def pick_block(count, most):
    best = 1
    for candidate in range(1, count + 1):
        if count % candidate == 0 and candidate <= most:
            best = candidate
    return best


def correlate(rows, cols, table, lag_vals, ratio, scale):
    row_spec, row_ints = rows
    col_spec, col_ints = cols
    nrows = row_spec.shape[0]
    ncols = col_spec.shape[0]
    segs = col_spec.shape[1]
    bins = col_spec.shape[3]
    lags = table.shape[1]
    col_flat = col_spec.reshape(ncols, 2 * segs, bins)
    turned = jnp.stack((-col_spec[:, :, 1], col_spec[:, :, 0]), axis=2).reshape(
        ncols, 2 * segs, bins
    )
    bstack = jnp.stack([col_flat, turned], axis=1)
    col_mask = col_ints[:, :segs].astype(jnp.float32)
    col_pos = col_ints[:, segs].astype(jnp.float32)
    block = pick_block(nrows, max(1, 1024 // ncols))

    def one_block(args):
        spec_blk, int_blk = args
        cross = jnp.einsum(
            "itf,jctf->ijcf", spec_blk, bstack, preferred_element_type=jnp.float32
        ).astype(jnp.bfloat16)
        raw = jnp.dot(
            cross.reshape(block * ncols, 2 * bins), table, preferred_element_type=jnp.float32
        ).reshape(block, ncols, lags)
        count = jnp.dot(
            int_blk[:, :segs].astype(jnp.float32), col_mask.T, precision=lax.Precision.HIGHEST
        )
        dist = jnp.abs(int_blk[:, segs].astype(jnp.float32)[:, None] - col_pos[None, :])
        span = 1.0 + dist * ratio
        taper = 1.0 / (1.0 + (lag_vals / span[:, :, None]) ** 2)
        norm = 1.0 / (scale * jnp.maximum(count, 1.0))
        return (raw * taper * norm[:, :, None]).astype(jnp.bfloat16)

    spec_rows = row_spec.reshape(nrows // block, block, 2 * segs, bins)
    int_rows = row_ints.reshape(nrows // block, block, row_ints.shape[1])
    out = lax.map(one_block, (spec_rows, int_rows))
    return out.reshape(nrows, ncols, lags)


def body(spectra, seg_mask, chan_pos):
    masked = spectra * seg_mask.astype(jnp.bfloat16)[:, :, None, None]
    ints = jnp.concatenate([seg_mask, chan_pos[:, None]], axis=1)
    chans = spectra.shape[0] * lax.axis_size("grp") * lax.axis_size("mem")
    table, lag_vals = make_table(BINS, LAGS)
    ratio = LAGS / chans
    scale = math.sqrt(BINS)
    cols = (
        lax.all_gather(masked, "grp", axis=0, tiled=True),
        lax.all_gather(ints, "grp", axis=0, tiled=True),
    )
    result = correlate(
        lax.all_gather((masked, ints), "mem", axis=0, tiled=True),
        cols,
        table,
        lag_vals,
        ratio,
        scale,
    )
    return result.reshape(result.shape[0], lax.axis_size("grp"), spectra.shape[0], LAGS)


def solution(mesh):
    in_specs = (P(("grp", "mem"), None, None, None), P(("grp", "mem"), None), P(("grp", "mem")))
    out_specs = P("grp", None, "mem", None)
    return jax.shard_map(body, mesh=mesh, in_specs=in_specs, out_specs=out_specs, check_vma=False)
```

profile of v0, /device:TPU:0, one launch (start us, length us, event | category | flops | bytes accessed | tf_op | source)
XLA Modules:
  0.0 105.4 jit_solution(3508888565890975375)
XLA Ops:
  6.5 0.7 convert_element_type.51
  7.2 1.6 %copy_multiply_fusion = bf16[4,8,2,1024]{3,1,2,0:T(8,128)(2,1)} fusion(bf16[4,8,2,1024]{3,2,1,0:T(2,128)(2,1)} %param.3, bf16[4,8]{1,0:T(4,128)(2,1)S(1)} %convert_element_type.51), kind=kLoop, calls=%fused_computation.30 | loop fusion | flops 65536 | bytes 262208 | tf_op jit(solution)/shard_map/mul | solution.py:70
  8.9 17.6 %all_gather.12 = bf16[16,8,2,1024]{3,1,2,0:T(8,128)(2,1)S(1)} all-gather(bf16[4,8,2,1024]{3,1,2,0:T(8,128)(2,1)} %copy_multiply_fusion), channel_id=1, replica_groups=mesh['grp'=4,'mem'=8] {'grp'}, dimensions={0}, use_global_device_ids=true | all-gather | bytes 655360 | tf_op jit(solution)/shard_map/all_gather | solution.py:77
  26.5 0.3 copy.38
  26.9 4.9 %copy.42 = bf16[16,1,16,1024]{2,0,1,3:T(8,128)(2,1)} copy(bf16[16,1,16,1024]{3,0,2,1:T(8,128)(2,1)S(1)} %bitcast.24) | data formatting | bytes 1048576 | tf_op jit(solution)/shard_map/stack;reshape | solution.py:41
  31.8 4.9 %copy.41 = bf16[16,1,16,1024]{2,0,1,3:T(8,128)(2,1)} copy(bf16[16,1,16,1024]{3,0,2,1:T(8,128)(2,1)S(1)} %bitcast.22) | data formatting | bytes 1048576 | tf_op jit(solution)/shard_map/stack;reshape | solution.py:41
  36.7 0.1 copy.45
  36.8 0.1 add_bitcast_fusion
  36.9 8.9 %all-gather = s32[8,4,9]{2,1,0:T(4,128)S(1)} all-gather(s32[1,4,9]{2,1,0:T(4,128)S(1)} %add_bitcast_fusion), channel_id=1, replica_groups=mesh['grp'=4,'mem'=8] {'mem'}, dimensions={0}, use_global_device_ids=true | all-gather | bytes 1296 | tf_op jit(solution)/shard_map/all_gather | solution.py:81
  45.8 0.1 slice_convert_fusion.2
  45.8 0.1 copy.53
  45.9 12.2 %all-gather.1 = s32[4,4,9]{2,1,0:T(4,128)S(1)} all-gather(s32[1,4,9]{2,1,0:T(4,128)S(1)} %add_bitcast_fusion), channel_id=1, replica_groups=mesh['grp'=4,'mem'=8] {'grp'}, dimensions={0}, use_global_device_ids=true | all-gather | bytes 720 | tf_op jit(solution)/shard_map/all_gather | solution.py:78
  58.1 0.1 slice_convert_fusion.5
  58.1 0.1 copy.54
  58.2 0.1 abs_add_fusion
  58.3 0.1 copy.48
  58.4 0.2 fusion.9
  58.5 0.1 copy.49
  58.6 2.2 %cosine_convert_fusion = (bf16[1024,128]{1,0:T(8,128)(2,1)S(1)}, bf16[1024,128]{1,0:T(8,128)(2,1)S(1)}) fusion(s32[128]{0:T(128)S(1)} %iota_add_fusion), kind=kLoop, calls=%fused_computation.22 | loop fusion | flops 2228224 | bytes 524800 | tf_op jit(solution)/shard_map/convert
  60.9 7.7 %copy.43 = bf16[32,8,2,1024]{0,2,1,3:T(2,128)(2,1)} copy(bf16[32,8,2,1024]{3,1,2,0:T(8,128)(2,1)} %all-gather.4.cloned.1.call-done) | data formatting | bytes 2097152 | tf_op jit(solution)/shard_map/all_gather | solution.py:81
  68.6 10.2 %convert_bitcast_fusion = bf16[32,16,2,1024]{0,1,2,3:T(8,128)(2,1)} fusion(bf16[32,16,1024,1]{0,1,3,2:T(8,128)(2,1)} %bitcast.23, bf16[16,1,16,1024]{2,0,1,3:T(8,128)(2,1)} %copy.42, bf16[16,1,16,1024]{2,0,1,3:T(8,128)(2,1)} %copy.41), kind=kOutput, calls=%fused_computation.4 | convolution fusion | flops 35127296 | bytes 4194304 | tf_op jit(solution)/shard_map/while/body/eval_jaxpr/itf,jctf->ijcf/dot_general | solution.py:48
  78.8 14.0 %copy.44 = bf16[32,16,2,1024]{3,2,1,0:T(2,128)(2,1)S(1)} copy(bf16[32,16,2,1024]{0,1,2,3:T(8,128)(2,1)} %convert_bitcast_fusion) | data formatting | bytes 4194304 | tf_op jit(solution)/shard_map/while/body/eval_jaxpr/convert_element_type | solution.py:50
  92.8 2.8 %dot_general.15 = bf16[32,16,2048]{2,1,0:T(8,128)(2,1)} reshape(bf16[32,16,2,1024]{3,2,1,0:T(2,128)(2,1)S(1)} %copy.44) | data formatting | bytes 4194304 | tf_op jit(solution)/shard_map/while/body/eval_jaxpr/dot_general | solution.py:51
  95.6 3.0 %fusion.7 = bf16[32,16,128]{2,1,0:T(8,128)(2,1)} fusion(bf16[32,16,2048]{2,1,0:T(8,128)(2,1)} %dot_general.15, bf16[1024,128]{1,0:T(8,128)(2,1)S(1)} %get-tuple-element.24, bf16[1024,128]{1,0:T(8,128)(2,1)S(1)} %get-tuple-element.23, f32[32,16]{1,0:T(8,128)S(1)} %copy.49, f32[32,16]{1,0:T(8,128)S(1)} %copy.48, f32[128]{0:T(128)S(1)} %fusion.20), kind=kOutput, calls=%fused_computation.7 | convolution fusion | flops 269942784 | bytes 2757120 | tf_op jit(solution)/shard_map/while/body/eval_jaxpr/dot_general | solution.py:51
  (11 shorter events, 0.1 us)
Async XLA Ops:
  6.5 54.4 %all-gather.4.cloned.1.call-start = ((), (), s32[]{:S(2)}) async-start(), calls=%async_computation | async-start | bytes 1179648 | tf_op jit(solution)/shard_map/all_gather | solution.py:81
  26.9 9.8 %copy-start.1 = (s32[4]{0:T(128)S(1)}, s32[4]{0:T(128)}, u32[]{:S(2)}) copy-start(s32[4]{0:T(128)} %param.5) | copy-start | bytes 52
  26.9 9.9 %copy-start = (s32[4,8]{1,0:T(4,128)S(1)}, s32[4,8]{1,0:T(4,128)}, u32[]{:S(2)}) copy-start(s32[4,8]{1,0:T(4,128)} %param.4) | copy-start | bytes 388
Sparse Core Ops, SparseCore 0:
  9.2 26.1 all-gather.3
where the time goes:
time: 106 us; the launch traced here: 105 us
  blocking collectives  38.6 us (36%)
  local copies, waits for them, and re-layouts  35 us (33%)
  between operations  13.5 us (13%)
  matrix products  13.3 us (13%)
  other arithmetic  4.95 us (5%)
    all_gather x1, blocking collectives, body(): lax.all_gather(masked, 'grp', axis=0, tiled=True)  17.6 us
    convert_element_type x1, local copies, waits for them, and re-layouts, one_block(): cross = jnp.einsum('itf,jctf->ijcf', spec_blk, bstack, preferred_element_...  14 us
    all_gather x1, blocking collectives, body(): lax.all_gather(ints, 'grp', axis=0, tiled=True)  12.2 us
    dot_general x1, matrix products, one_block(): jnp.einsum('itf,jctf->ijcf', spec_blk, bstack, preferred_element_type=jnp...  10.2 us
    another operation x2, local copies, waits for them, and re-layouts, correlate(): bstack = jnp.stack([col_flat, turned], axis=1)  9.81 us
    all_gather x1, blocking collectives, body(): lax.all_gather((masked, ints), 'mem', axis=0, tiled=True)  8.89 us
    all_gather x1, local copies, waits for them, and re-layouts, body(): lax.all_gather((masked, ints), 'mem', axis=0, tiled=True)  7.69 us
    dot_general x1, matrix products, one_block(): jnp.dot(cross.reshape(block * ncols, 2 * bins), table, preferred_element_...  2.96 us
  transfers between devices with their start and end apart: 1, of which 0 were waited for; matrix products, arithmetic and copies ran while one was open for 13% of the time, Pallas kernels for 0%

commit v1 on v0

--- a/solution.py
+++ b/solution.py
@@ -6,6 +6,19 @@
 
 BINS = 1024
 LAGS = 128
+
+
+def ring_gather(value, axis, dim):
+    ways = lax.axis_size(axis)
+    up = [(d, (d + 1) % ways) for d in range(ways)]
+    down = [(d, (d - 1) % ways) for d in range(ways)]
+    earlier, later = ([value], [value])
+    for _ in range(ways // 2):
+        earlier.append(lax.ppermute(earlier[-1], axis, up))
+    for _ in range((ways - 1) // 2):
+        later.append(lax.ppermute(later[-1], axis, down))
+    line = jnp.concatenate([*earlier[::-1], *later[1:]], axis=dim)
+    return jnp.roll(line, (lax.axis_index(axis) - ways // 2) * value.shape[dim], axis=dim)
 
 
 def make_table(bins, lags):
@@ -73,10 +86,7 @@
     table, lag_vals = make_table(BINS, LAGS)
     ratio = LAGS / chans
     scale = math.sqrt(BINS)
-    cols = (
-        lax.all_gather(masked, "grp", axis=0, tiled=True),
-        lax.all_gather(ints, "grp", axis=0, tiled=True),
-    )
+    cols = (ring_gather(masked, "grp", 0), lax.all_gather(ints, "grp", axis=0, tiled=True))
     result = correlate(
         lax.all_gather((masked, ints), "mem", axis=0, tiled=True),
         cols,

time: 106 us -> 103 us (0.972)
  blocking collectives: 38.6 us -> 20.9 us
  waiting for transfers between devices: 0.04 us -> 6.54 us
  starting transfers between devices: 0.01 us -> 5.23 us
  local copies, waits for them, and re-layouts: 35 us -> 37.2 us
    all_gather x1 -> x0, blocking collectives: 17.6 us -> none  [body(): lax.all_gather(masked, 'grp', axis=0, tiled=True)]
    ppermute x0 -> x3, waiting for transfers between devices: none -> 6.52 us  [the longest x2 6.52 us: ring_gather(): earlier.append(lax.ppermute(earlier[-1], axis, up))]
    ppermute x0 -> x3, starting transfers between devices: none -> 5.23 us  [the longest x2 3.13 us: ring_gather(): earlier.append(lax.ppermute(earlier[-1], axis, up))]
  transfers between devices with their start and end apart: 1 -> 4, of which waited for: 0 -> 1; matrix products, arithmetic and copies ran while one was open for 13% -> 16% of each run, Pallas kernels for 0% -> 0%
where the time goes in v1:
time: 103 us; the launch traced here: 102 us
  local copies, waits for them, and re-layouts  37.2 us (36%)
  blocking collectives  20.9 us (20%)
  between operations  13.5 us (13%)
  matrix products  13.3 us (13%)
  waiting for transfers between devices  6.54 us (6%)
  starting transfers between devices  5.23 us (5%)
  other arithmetic  5.18 us (5%)
    convert_element_type x1, local copies, waits for them, and re-layouts, one_block(): cross = jnp.einsum('itf,jctf->ijcf', spec_blk, bstack, preferred_element_...  14 us
    all_gather x1, blocking collectives, body(): lax.all_gather(ints, 'grp', axis=0, tiled=True)  11.9 us
    dot_general x1, matrix products, one_block(): jnp.einsum('itf,jctf->ijcf', spec_blk, bstack, preferred_element_type=jnp...  10.2 us
    another operation x2, local copies, waits for them, and re-layouts, correlate(): bstack = jnp.stack([col_flat, turned], axis=1)  9.8 us
    all_gather x1, blocking collectives, body(): lax.all_gather((masked, ints), 'mem', axis=0, tiled=True)  9.05 us
    all_gather x1, local copies, waits for them, and re-layouts, body(): lax.all_gather((masked, ints), 'mem', axis=0, tiled=True)  7.68 us
    ppermute x2, waiting for transfers between devices, ring_gather(): earlier.append(lax.ppermute(earlier[-1], axis, up))  6.52 us
    ppermute x2, starting transfers between devices, ring_gather(): earlier.append(lax.ppermute(earlier[-1], axis, up))  3.13 us
  transfers between devices with their start and end apart: 4, of which 1 were waited for; matrix products, arithmetic and copies ran while one was open for 16% of the time, Pallas kernels for 0%

profile of v1, /device:TPU:0, one launch (start us, length us, event | category | flops | bytes accessed | tf_op | source)
XLA Modules:
  0.0 101.9 jit_solution(4156174885810586245)
XLA Ops:
  6.5 0.7 convert_element_type.51
  7.2 0.1 copy.36
  7.3 1.0 %copy_multiply_fusion = bf16[4,8,2,1024]{3,0,2,1:T(4,128)(2,1)S(1)} fusion(bf16[4,8,2,1024]{3,2,1,0:T(2,128)(2,1)} %param.3, bf16[4,8]{0,1:T(8,128)(2,1)S(1)} %copy.36), kind=kLoop, calls=%fused_computation.30 | loop fusion | flops 65536 | bytes 262208 | tf_op jit(solution)/shard_map/mul | solution.py:83
  8.3 3.1 %collective-permute-start = (bf16[4,8,2,1024]{3,0,2,1:T(4,128)(2,1)S(1)}, bf16[4,8,2,1024]{3,0,2,1:T(4,128)(2,1)S(1)}, u32[]{:S(2)}, u32[]{:S(2)}) collective-permute-start(bf16[4,8,2,1024]{3,0,2,1:T(4,128)(2,1)S(1)} %copy_multiply_fusion), channel_id=1, source_target_pairs={{0,8},{8,16},{16,24},{24,0},{1,9},{9,17},{17,25},{25,1},{2,10},{10... | collective-permute-start | bytes 393224 | tf_op jit(solution)/shard_map/ppermute | solution.py:17
  11.4 2.1 %collective-permute-start.2 = (bf16[4,8,2,1024]{3,0,2,1:T(4,128)(2,1)S(1)}, bf16[4,8,2,1024]{3,0,2,1:T(4,128)(2,1)S(1)}, u32[]{:S(2)}, u32[]{:S(2)}) collective-permute-start(bf16[4,8,2,1024]{3,0,2,1:T(4,128)(2,1)S(1)} %copy_multiply_fusion), channel_id=1, source_target_pairs={{0,24},{8,0},{16,8},{24,16},{1,25},{9,1},{17,9},{25,17},{2,26},{10... | collective-permute-start | bytes 393224 | tf_op jit(solution)/shard_map/ppermute | solution.py:19
  13.5 0.7 copy.40
  14.3 0.7 copy.43
  15.0 0.8 add_bitcast_fusion
  15.8 9.0 %all-gather = s32[8,4,9]{2,1,0:T(4,128)S(1)} all-gather(s32[1,4,9]{2,1,0:T(4,128)S(1)} %add_bitcast_fusion), channel_id=1, replica_groups=mesh['grp'=4,'mem'=8] {'mem'}, dimensions={0}, use_global_device_ids=true | all-gather | bytes 1296 | tf_op jit(solution)/shard_map/all_gather | solution.py:91
  25.0 11.9 %all-gather.1 = s32[4,4,9]{2,1,0:T(4,128)S(1)} all-gather(s32[1,4,9]{2,1,0:T(4,128)S(1)} %add_bitcast_fusion), channel_id=1, replica_groups=mesh['grp'=4,'mem'=8] {'grp'}, dimensions={0}, use_global_device_ids=true | all-gather | bytes 720 | tf_op jit(solution)/shard_map/all_gather | solution.py:89
  36.9 0.1 copy.52
  37.0 2.2 %cosine_convert_fusion = (bf16[1024,128]{1,0:T(8,128)(2,1)S(1)}, bf16[1024,128]{1,0:T(8,128)(2,1)S(1)}) fusion(s32[128]{0:T(128)S(1)} %iota_add_fusion), kind=kLoop, calls=%fused_computation.22 | loop fusion | flops 2228224 | bytes 524800 | tf_op jit(solution)/shard_map/convert
  39.2 0.1 fusion.9
  39.7 6.5 %collective-permute-done.1 = bf16[4,8,2,1024]{3,0,2,1:T(4,128)(2,1)S(1)} collective-permute-done((bf16[4,8,2,1024]{3,0,2,1:T(4,128)(2,1)S(1)}, bf16[4,8,2,1024]{3,0,2,1:T(4,128)(2,1)S(1)}, u32[]{:S(2)}, u32[]{:S(2)}) %collective-permute-start.1) | collective-permute-done | bytes 131104 | tf_op jit(solution)/shard_map/ppermute | solution.py:17
  46.2 0.9 concatenate.13
  47.1 0.2 dynamic-slice_negate_fusion
  47.4 4.9 %copy.39 = bf16[16,1,16,1024]{2,0,1,3:T(8,128)(2,1)} copy(bf16[16,1,16,1024]{3,0,2,1:T(8,128)(2,1)S(1)} %bitcast.23) | data formatting | bytes 1048576 | tf_op jit(solution)/shard_map/stack;reshape | solution.py:54
  52.3 0.2 constant_dynamic-slice_fusion.1
  52.5 4.9 %copy.38 = bf16[16,1,16,1024]{2,0,1,3:T(8,128)(2,1)} copy(bf16[16,1,16,1024]{3,0,2,1:T(8,128)(2,1)S(1)} %bitcast.24) | data formatting | bytes 1048576 | tf_op jit(solution)/shard_map/stack;reshape | solution.py:54
  57.4 7.7 %copy.41 = bf16[32,8,2,1024]{0,2,1,3:T(2,128)(2,1)} copy(bf16[32,8,2,1024]{3,1,2,0:T(8,128)(2,1)} %all-gather.4.cloned.1.call-done) | data formatting | bytes 2097152 | tf_op jit(solution)/shard_map/all_gather | solution.py:91
  65.1 10.2 %convert_bitcast_fusion = bf16[32,16,2,1024]{0,1,2,3:T(8,128)(2,1)} fusion(bf16[32,16,1024,1]{0,1,3,2:T(8,128)(2,1)} %bitcast.22, bf16[16,1,16,1024]{2,0,1,3:T(8,128)(2,1)} %copy.39, bf16[16,1,16,1024]{2,0,1,3:T(8,128)(2,1)} %copy.38), kind=kOutput, calls=%fused_computation.4 | convolution fusion | flops 35127296 | bytes 4194304 | tf_op jit(solution)/shard_map/while/body/eval_jaxpr/itf,jctf->ijcf/dot_general | solution.py:61
  75.3 14.0 %copy.42 = bf16[32,16,2,1024]{3,2,1,0:T(2,128)(2,1)S(1)} copy(bf16[32,16,2,1024]{0,1,2,3:T(8,128)(2,1)} %convert_bitcast_fusion) | data formatting | bytes 4194304 | tf_op jit(solution)/shard_map/while/body/eval_jaxpr/convert_element_type | solution.py:63
  89.3 2.8 %dot_general.15 = bf16[32,16,2048]{2,1,0:T(8,128)(2,1)} reshape(bf16[32,16,2,1024]{3,2,1,0:T(2,128)(2,1)S(1)} %copy.42) | data formatting | bytes 4194304 | tf_op jit(solution)/shard_map/while/body/eval_jaxpr/dot_general | solution.py:64
  92.1 3.0 %fusion.7 = bf16[32,16,128]{2,1,0:T(8,128)(2,1)} fusion(bf16[32,16,2048]{2,1,0:T(8,128)(2,1)} %dot_general.15, bf16[1024,128]{1,0:T(8,128)(2,1)S(1)} %get-tuple-element.24, bf16[1024,128]{1,0:T(8,128)(2,1)S(1)} %get-tuple-element.23, f32[32,16]{1,0:T(8,128)S(1)} %copy.47, f32[32,16]{1,0:T(8,128)S(1)} %copy.46, f32[128]{0:T(128)S(1)} %fusion.20), kind=kOutput, calls=%fused_computation.7 | convolution fusion | flops 269942784 | bytes 2757120 | tf_op jit(solution)/shard_map/while/body/eval_jaxpr/dot_general | solution.py:64
  (15 shorter events, 0.6 us)
Async XLA Ops:
  6.5 50.9 %all-gather.4.cloned.1.call-start = ((), (), s32[]{:S(2)}) async-start(), calls=%async_computation | async-start | bytes 1179648 | tf_op jit(solution)/shard_map/all_gather | solution.py:91
  8.3 31.0 %collective-permute-start = (bf16[4,8,2,1024]{3,0,2,1:T(4,128)(2,1)S(1)}, bf16[4,8,2,1024]{3,0,2,1:T(4,128)(2,1)S(1)}, u32[]{:S(2)}, u32[]{:S(2)}) collective-permute-start(bf16[4,8,2,1024]{3,0,2,1:T(4,128)(2,1)S(1)} %copy_multiply_fusion), channel_id=1, source_target_pairs={{0,8},{8,16},{16,24},{24,0},{1,9},{9,17},{17,25},{25,1},{2,10},{10... | collective-permute-start | bytes 393224 | tf_op jit(solution)/shard_map/ppermute | solution.py:17
  11.4 28.3 %collective-permute-start.2 = (bf16[4,8,2,1024]{3,0,2,1:T(4,128)(2,1)S(1)}, bf16[4,8,2,1024]{3,0,2,1:T(4,128)(2,1)S(1)}, u32[]{:S(2)}, u32[]{:S(2)}) collective-permute-start(bf16[4,8,2,1024]{3,0,2,1:T(4,128)(2,1)S(1)} %copy_multiply_fusion), channel_id=1, source_target_pairs={{0,24},{8,0},{16,8},{24,16},{1,25},{9,1},{17,9},{25,17},{2,26},{10... | collective-permute-start | bytes 393224 | tf_op jit(solution)/shard_map/ppermute | solution.py:19
  39.4 6.8 %collective-permute-start.1 = (bf16[4,8,2,1024]{3,0,2,1:T(4,128)(2,1)S(1)}, bf16[4,8,2,1024]{3,0,2,1:T(4,128)(2,1)S(1)}, u32[]{:S(2)}, u32[]{:S(2)}) collective-permute-start(bf16[4,8,2,1024]{3,0,2,1:T(4,128)(2,1)S(1)} %collective-permute-done), channel_id=1, source_target_pairs={{0,8},{8,16},{16,24},{24,0},{1,9},{9,17},{17,25},{25,1},{2,10},{10... | collective-permute-start | bytes 393224 | tf_op jit(solution)/shard_map/ppermute | solution.py:17
Sparse Core Ops, SparseCore 0:
  14.4 23.0 all-gather.3
